TPU v7x, 256 devices: a whole 4x4x8 slice. The times are simulated.
256 devices in a mesh: rows: 32 (over z, x), rhs: 8 (over y, core).
Axes of the slice: x: 4, y: 4, z: 8, core: 2. Of those that a mesh axis runs over, the one named last changes fastest.
Arguments:
- right_side: float32 [32768, 1024], P('rows', 'rhs'), may hold values from -6 to 6
- leaf_blocks: bfloat16 [128, 2, 256, 256], P('rows'), may hold values from -0.25 to 0.25
- out_basis: bfloat16 [128, 2, 256, 128], P('rows'), may hold values from -0.375 to 0.375
- in_basis: bfloat16 [128, 2, 256, 128], P('rows'), may hold values from -0.25 to 0.25
- couplings: bfloat16 [128, 7, 2, 128, 128], P('rows'), may hold values from -6 to 6
Outputs:
- solution: float32 [2, 32768, 1024], P(None, 'rows', 'rhs')
All inputs are finite; a program needn't handle non-finite values.
Results may differ from a plain program's by a relative error of at most 0.0043.
Values sent between devices are 32-bit elements; how exact they have to be, the bound alone decides.
No kernel may reach another device: no remote copies, remote signals or barrier semaphores. Data moves between devices by JAX's collectives and lax.ppermute only.
A program may use at most 64 MiB of HBM per device.

v0:
```python
import math
import jax
import jax.numpy as jnp
from jax import lax
from jax.sharding import PartitionSpec as P


def dft_table(length, phase_sign):
    indices = jnp.arange(length, dtype=jnp.int32)
    product = indices[:, None] * indices[None, :] % length
    angles = 2.0 * math.pi / length * product.astype(jnp.float32)
    return (jnp.cos(angles), phase_sign * jnp.sin(angles))


def exact_mix(pattern, left_re, left_im, right_re, right_im):
    highest = lax.Precision.HIGHEST
    real_part = jnp.einsum(pattern, left_re, right_re, precision=highest) - jnp.einsum(
        pattern, left_im, right_im, precision=highest
    )
    imag_part = jnp.einsum(pattern, left_re, right_im, precision=highest) + jnp.einsum(
        pattern, left_im, right_re, precision=highest
    )
    return (real_part, imag_part)


def narrow_mix(pattern, left_re, left_im, right_re, right_im):
    real_part = jnp.einsum(
        pattern, left_re, right_re, preferred_element_type=jnp.float32
    ) - jnp.einsum(pattern, left_im, right_im, preferred_element_type=jnp.float32)
    imag_part = jnp.einsum(
        pattern, left_re, right_im, preferred_element_type=jnp.float32
    ) + jnp.einsum(pattern, left_im, right_re, preferred_element_type=jnp.float32)
    return (real_part, imag_part)


def local_dft(values_re, values_im, phase_sign):
    length, columns = values_re.shape
    first = 2 ** ((length.bit_length() - 1) // 2)
    second = length // first
    table_re, table_im = dft_table(first, phase_sign)
    grid_re = values_re.reshape(first, second, columns)
    highest = lax.Precision.HIGHEST
    if values_im is None:
        part_re = jnp.einsum("kh,hlc->klc", table_re, grid_re, precision=highest)
        part_im = jnp.einsum("kh,hlc->klc", table_im, grid_re, precision=highest)
    else:
        grid_im = values_im.reshape(first, second, columns)
        part_re, part_im = exact_mix("kh,hlc->klc", table_re, table_im, grid_re, grid_im)
    low_index = jnp.arange(first, dtype=jnp.int32)
    high_index = jnp.arange(second, dtype=jnp.int32)
    twist = (low_index[:, None] * high_index[None, :] % length).astype(jnp.float32) * (
        2.0 * math.pi / length
    )
    twist_re = jnp.cos(twist)[:, :, None]
    twist_im = phase_sign * jnp.sin(twist)[:, :, None]
    turned_re = part_re * twist_re - part_im * twist_im
    turned_im = part_re * twist_im + part_im * twist_re
    outer_re, outer_im = dft_table(second, phase_sign)
    result_re, result_im = exact_mix("jl,klc->jkc", outer_re, outer_im, turned_re, turned_im)
    return (result_re.reshape(length, columns), result_im.reshape(length, columns))


def sibling_sum(values, group):
    count, rank_size, columns = values.shape
    grouped = values.reshape(count // (2 * group), 2, group, rank_size, columns).sum(axis=2)
    swapped = grouped[:, ::-1]
    spread = jnp.broadcast_to(
        swapped[:, :, None], (count // (2 * group), 2, group, rank_size, columns)
    )
    return spread.reshape(count, rank_size, columns)


def shards(right_side, leaf_blocks, out_basis, in_basis, couplings):
    rows_count = lax.axis_size("rows")
    device = lax.axis_index("rows")
    length, columns = right_side.shape
    full_order = length * rows_count
    band_size = length // rows_count
    norm_factor = 1.0 / math.sqrt(full_order)
    positions = jnp.arange(length, dtype=jnp.int32)
    phases = (device * positions % full_order).astype(jnp.float32) * (2.0 * math.pi / full_order)
    phase_re = jnp.cos(phases)[:, None]
    phase_im = jnp.sin(phases)[:, None]
    local_re, local_im = local_dft(right_side, None, -1.0)
    turned = jnp.stack(
        [local_re * phase_re + local_im * phase_im, local_im * phase_re - local_re * phase_im]
    )
    turned = turned.reshape(2, rows_count, band_size, columns)
    across_re, across_im = dft_table(rows_count, -1.0)
    blocks = lax.all_to_all(turned, "rows", split_axis=1, concat_axis=1, tiled=True)
    mixed_re, mixed_im = exact_mix("jd,dqc->jqc", across_re, across_im, blocks[0], blocks[1])
    ordered = (jnp.stack([mixed_re, mixed_im]) * norm_factor).astype(jnp.bfloat16)
    leaf_count = out_basis.shape[0]
    leaf_size = out_basis.shape[2]
    rank_size = out_basis.shape[3]
    level_count = couplings.shape[1]
    inner_levels = leaf_count.bit_length() - 1
    up_levels = rows_count.bit_length() - 1
    leaves = ordered.reshape(2, leaf_count, leaf_size, columns)
    coeff_re, coeff_im = narrow_mix(
        "lar,lac->lrc", in_basis[:, 0], -in_basis[:, 1], leaves[0], leaves[1]
    )
    inner_re = []
    inner_im = []
    for level_index in range(inner_levels):
        group = 2**level_index
        weight = (2.0 * rank_size * level_count * group) ** (-0.5)
        inner_re.append((weight * sibling_sum(coeff_re, group)).astype(jnp.bfloat16))
        inner_im.append((weight * sibling_sum(coeff_im, group)).astype(jnp.bfloat16))
    field_re, field_im = narrow_mix(
        "ltrs,tlsc->lrc",
        couplings[:, :inner_levels, 0],
        couplings[:, :inner_levels, 1],
        jnp.stack(inner_re),
        jnp.stack(inner_im),
    )
    totals = jnp.stack([jnp.sum(coeff_re, axis=0), jnp.sum(coeff_im, axis=0)])
    every = lax.all_gather(totals[None], "rows", axis=0, tiled=True)
    device_ids = jnp.arange(rows_count, dtype=jnp.int32)
    bit_ids = jnp.arange(up_levels, dtype=jnp.int32)
    partner_group = jnp.bitwise_xor(jnp.right_shift(device, bit_ids), 1)
    member = (
        jnp.right_shift(device_ids[None, :], bit_ids[:, None]) == partner_group[:, None]
    ).astype(jnp.float32)
    groups = jnp.einsum("ud,dkrc->ukrc", member, every, precision=lax.Precision.HIGHEST)
    scales = jnp.asarray(
        [
            (2.0 * rank_size * level_count * 2 ** (inner_levels + bit_index)) ** (-0.5)
            for bit_index in range(up_levels)
        ],
        jnp.float32,
    )
    across = (groups * scales[:, None, None, None]).astype(jnp.bfloat16)
    cross_re, cross_im = narrow_mix(
        "lurs,usc->lrc",
        couplings[:, inner_levels:, 0],
        couplings[:, inner_levels:, 1],
        across[:, 0],
        across[:, 1],
    )
    field_low_re = (field_re + cross_re).astype(jnp.bfloat16)
    field_low_im = (field_im + cross_im).astype(jnp.bfloat16)
    far_re, far_im = narrow_mix(
        "lar,lrc->lac", out_basis[:, 0], out_basis[:, 1], field_low_re, field_low_im
    )
    own_re, own_im = narrow_mix(
        "lab,lbc->lac", leaf_blocks[:, 0], leaf_blocks[:, 1], leaves[0], leaves[1]
    )
    image = jnp.stack([own_re + far_re, own_im + far_im])
    image = image.reshape(2, rows_count, band_size, columns)
    back_re, back_im = dft_table(rows_count, 1.0)
    spectral_re, spectral_im = exact_mix("jd,dqc->jqc", back_re, back_im, image[0], image[1])
    blocks = lax.all_to_all(
        jnp.stack([spectral_re, spectral_im]), "rows", split_axis=1, concat_axis=1, tiled=True
    )
    count = blocks.shape[3]
    flat_re = blocks[0].reshape(length, count)
    flat_im = blocks[1].reshape(length, count)
    rolled_re = flat_re * phase_re - flat_im * phase_im
    rolled_im = flat_re * phase_im + flat_im * phase_re
    result_re, result_im = local_dft(rolled_re, rolled_im, 1.0)
    return jnp.stack([result_re, result_im]) * norm_factor


def solution(mesh):
    placed = (
        P("rows", "rhs"),
        P("rows", None, None, None),
        P("rows", None, None, None),
        P("rows", None, None, None),
        P("rows", None, None, None, None),
    )
    return jax.shard_map(
        shards, mesh=mesh, in_specs=placed, out_specs=P(None, "rows", "rhs"), check_vma=False
    )
```

profile of v0, /device:TPU:2, one launch (start us, length us, event | category | flops | bytes accessed | tf_op | source)
XLA Modules:
  0.0 204.1 jit_solution(9726625276925699508)
XLA Ops:
  8.5 1.0 multiply_add_fusion.2
  9.5 0.9 fusion.57
  11.3 0.9 convolution_add_fusion.5
  12.2 1.0 add_bitcast_fusion
  14.0 39.5 %all_to_all.10 = f32[2,32,32,128]{3,2,0,1:T(8,128)S(1)} all-to-all(f32[2,32,32,128]{3,2,0,1:T(8,128)S(1)} %copy.94), channel_id=1, replica_groups=mesh['rows'=32,'rhs'=8] {'rows'}, dimensions={1} | all-to-all | bytes 2097152 | tf_op jit(solution)/shard_map/all_to_all | solution.py:90
  53.5 0.9 fusion.43
  55.3 0.9 fusion.15
  56.2 0.9 fusion.14
  61.0 1.0 convolution_bitcast_fusion.2
  62.0 0.9 convolution_bitcast_fusion.6
  63.6 1.1 convolution_add_fusion.6
  64.7 1.1 convolution_subtract_fusion.6
  65.8 71.9 %all-gather.3.cloned.1.call-done = f32[64,128,128]{2,1,0:T(8,128)} async-done(((f32[2,128,128]{2,1,0:T(8,128)}), f32[64,128,128]{2,1,0:T(8,128)}) %all-gather.3.cloned.1.call-update) | async-done | bytes 4194320 | tf_op jit(solution)/shard_map/all_gather | solution.py:118
  137.7 5.8 %fusion.5 = bf16[5,2,128,128]{3,0,2,1:T(8,128)(2,1)S(1)} fusion(f32[32,2,128,128]{3,2,1,0:T(8,128)} %bitcast.317, f32[5]{0:T(128)S(1)} %copy-done.21, s32[5]{0:T(128)S(1)} %copy-done.22), kind=kOutput, calls=%fused_computation.3 | convolution fusion | flops 63242560 | bytes 4522024 | tf_op jit(solution)/shard_map/ud,dkrc->ukrc/dot_general | solution.py:125
  148.2 0.9 fusion.55
  151.9 1.6 copy.129
  153.5 7.6 %all-to-all-start.1 = ((f32[2,32,32,128]{3,2,0,1:T(8,128)}), f32[2,32,32,128]{3,2,0,1:T(8,128)S(1)}, u32[]{:S(2)}, u32[]{:S(2)}) async-start(f32[2,32,32,128]{3,2,0,1:T(8,128)} %copy.129), calls=%async_computation.1 | async-start | bytes 2097152 | tf_op jit(solution)/shard_map/all_to_all | solution.py:153
  161.3 25.3 %all-to-all-done.1 = f32[2,32,32,128]{3,2,0,1:T(8,128)S(1)} async-done(((f32[2,32,32,128]{3,2,0,1:T(8,128)}), f32[2,32,32,128]{3,2,0,1:T(8,128)S(1)}, u32[]{:S(2)}, u32[]{:S(2)}) %all-to-all-start.1) | async-done | bytes 1048608 | tf_op jit(solution)/shard_map/all_to_all | solution.py:153
  186.6 1.3 fusion.103
  187.9 1.3 fusion.102
  189.2 1.3 convolution_subtract_fusion.1
  190.6 1.4 multiply_subtract_fusion
  194.7 0.9 convolution_add_fusion
  196.2 1.1 maximum_multiply_fusion.1
  (109 shorter events, 19.5 us)
Async XLA Ops:
  6.5 1.0 copy-start
  6.5 131.2 %all-gather.3.cloned.1.call-start = ((), (), s32[]{:S(2)}) async-start(), calls=%async_computation.2 | async-start | bytes 4325376 | tf_op jit(solution)/shard_map/all_gather | solution.py:118
  6.8 3.6 %copy-start.19 = (f32[32,32]{0,1:T(8,128)}, f32[32,32]{0,1:T(8,128)S(1)}, u32[]{:S(2)}) copy-start(f32[32,32]{0,1:T(8,128)S(1)} %copy.85) | copy-start | bytes 12292
  7.6 4.6 %copy-start.7 = (f32[32,32]{0,1:T(8,128)}, f32[32,32]{0,1:T(8,128)S(1)}, u32[]{:S(2)}) copy-start(f32[32,32]{0,1:T(8,128)S(1)} %copy.90) | copy-start | bytes 12292
  57.1 1.0 copy-start.3
  59.0 1.9 copy-start.1
  60.8 2.1 %copy-start.2 = (bf16[4,2,256,256]{3,2,1,0:T(8,128)(2,1)S(1)}, bf16[4,2,256,256]{3,2,1,0:T(8,128)(2,1)}, u32[]{:S(2)}) copy-start(bf16[4,2,256,256]{3,2,1,0:T(8,128)(2,1)} %param.7) | copy-start | bytes 3145732
  60.9 2.3 %copy-start.9 = (bf16[2,2,128,128]{2,3,1,0:T(8,128)(2,1)}, bf16[2,2,128,128]{2,3,1,0:T(8,128)(2,1)S(1)}, u32[]{:S(2)}) copy-start(bf16[2,2,128,128]{2,3,1,0:T(8,128)(2,1)S(1)} %multiply_convert_fusion.1) | copy-start | bytes 393220
  60.9 2.6 %copy-start.11 = (bf16[2,2,128,128]{2,3,1,0:T(8,128)(2,1)}, bf16[2,2,128,128]{2,3,1,0:T(8,128)(2,1)S(1)}, u32[]{:S(2)}) copy-start(bf16[2,2,128,128]{2,3,1,0:T(8,128)(2,1)S(1)} %multiply_convert_fusion) | copy-start | bytes 393220
  61.0 2.6 %copy-start.13 = (bf16[2,2,128,128]{2,3,1,0:T(8,128)(2,1)}, bf16[2,2,128,128]{2,3,1,0:T(8,128)(2,1)S(1)}, u32[]{:S(2)}) copy-start(bf16[2,2,128,128]{2,3,1,0:T(8,128)(2,1)S(1)} %broadcast_in_dim.6) | copy-start | bytes 393220
  62.0 2.7 %copy-start.15 = (bf16[2,2,128,128]{2,3,1,0:T(8,128)(2,1)}, bf16[2,2,128,128]{2,3,1,0:T(8,128)(2,1)S(1)}, u32[]{:S(2)}) copy-start(bf16[2,2,128,128]{2,3,1,0:T(8,128)(2,1)S(1)} %broadcast_in_dim.7) | copy-start | bytes 393220
  63.6 74.2 %copy-start.21 = (f32[5]{0:T(128)S(1)}, f32[5]{0:T(128)}, u32[]{:S(2)}) copy-start(f32[5]{0:T(128)} %constant.88.clone) | copy-start | bytes 64
  63.6 74.2 %copy-start.22 = (s32[5]{0:T(128)S(1)}, s32[5]{0:T(128)}, u32[]{:S(2)}) copy-start(s32[5]{0:T(128)} %shift-right-arithmetic_xor_fusion) | copy-start | bytes 64
  144.4 1.1 copy-start.12
  144.4 1.1 copy-start.16
  144.4 1.1 copy-start.18
  144.8 1.0 copy-start.10
  144.8 1.1 copy-start.17
  145.2 1.1 copy-start.4
  145.6 1.2 copy-start.6
  146.5 1.1 copy-start.5
  153.5 33.1 %copy-start.8 = (f32[32,32]{0,1:T(8,128)S(1)}, f32[32,32]{0,1:T(8,128)}, u32[]{:S(2)}) copy-start(f32[32,32]{0,1:T(8,128)} %copy-done.7) | copy-start | bytes 12292
  153.5 33.0 %all-to-all-start.1 = ((f32[2,32,32,128]{3,2,0,1:T(8,128)}), f32[2,32,32,128]{3,2,0,1:T(8,128)S(1)}, u32[]{:S(2)}, u32[]{:S(2)}) async-start(f32[2,32,32,128]{3,2,0,1:T(8,128)} %copy.129), calls=%async_computation.1 | async-start | bytes 2097152 | tf_op jit(solution)/shard_map/all_to_all | solution.py:153
  187.9 2.6 %copy-start.20 = (f32[32,32]{0,1:T(8,128)S(1)}, f32[32,32]{0,1:T(8,128)}, u32[]{:S(2)}) copy-start(f32[32,32]{0,1:T(8,128)} %copy-done.19) | copy-start | bytes 12292
  (1 other events, 1.0 us)
Sparse Core Ops, SparseCore 0:
  60.3 77.4 all-gather.2
where the time goes:
time: 205 us; the launch traced here: 204 us
  waiting for transfers between devices  97.2 us (47%)
  blocking collectives  39.5 us (19%)
  matrix products  36.3 us (18%)
  between operations  14.1 us (7%)
  starting transfers between devices  7.6 us (4%)
  local copies, waits for them, and re-layouts  7.04 us (3%)
  other arithmetic  2.41 us (1%)
    all_gather x1, waiting for transfers between devices, shards(): every = lax.all_gather(totals[None], 'rows', axis=0, tiled=True)  71.9 us
    all_to_all x1, blocking collectives, shards(): lax.all_to_all(turned, 'rows', split_axis=1, concat_axis=1, tiled=True)  39.5 us
    all_to_all x1, waiting for transfers between devices, shards(): lax.all_to_all(jnp.stack([spectral_re, spectral_im]), 'rows', split_axis=...  25.3 us
    all_to_all x1, starting transfers between devices, shards(): lax.all_to_all(jnp.stack([spectral_re, spectral_im]), 'rows', split_axis=...  7.6 us
    dot_general x1, matrix products, shards(): jnp.einsum('ud,dkrc->ukrc', member, every, precision=lax.Precision.HIGHEST)  5.82 us
    dot_general x5, matrix products, exact_mix(): jnp.einsum(pattern, left_im, right_re, precision=highest)  5.04 us
    dot_general x5, matrix products, exact_mix(): jnp.einsum(pattern, left_im, right_im, precision=highest)  5.01 us
    dot_general x5, matrix products, exact_mix(): jnp.einsum(pattern, left_re, right_im, precision=highest)  4.87 us
  transfers between devices with their start and end apart: 2, of which 2 were waited for; matrix products, arithmetic and copies ran while one was open for 3% of the time, Pallas kernels for 0%

commit v1 on v0

--- a/solution.py
+++ b/solution.py
@@ -115,7 +115,13 @@
         jnp.stack(inner_im),
     )
     totals = jnp.stack([jnp.sum(coeff_re, axis=0), jnp.sum(coeff_im, axis=0)])
-    every = lax.all_gather(totals[None], "rows", axis=0, tiled=True)
+    m = totals[None]
+    every = jnp.concatenate(
+        lax.all_to_all(
+            jnp.stack(lax.axis_size("rows") * [m], 0), "rows", split_axis=0, concat_axis=0
+        ),
+        0,
+    )
     device_ids = jnp.arange(rows_count, dtype=jnp.int32)
     bit_ids = jnp.arange(up_levels, dtype=jnp.int32)
     partner_group = jnp.bitwise_xor(jnp.right_shift(device, bit_ids), 1)

time: 205 us -> 216 us (1.054)
  waiting for transfers between devices: 97.2 us -> 112 us
  between operations: 14.1 us -> 0.7 us
  starting transfers between devices: 7.6 us -> 14.1 us
  local copies, waits for them, and re-layouts: 7.04 us -> 11.2 us
    all_to_all x0 -> x1, waiting for transfers between devices: none -> 85.3 us  [shards(): lax.all_to_all(jnp.stack(lax.axis_size('rows') * [m], 0), 'rows', split_a...]
    all_gather x1 -> x0, waiting for transfers between devices: 71.9 us -> none  [shards(): every = lax.all_gather(totals[None], 'rows', axis=0, tiled=True)]
    all_to_all x0 -> x1, starting transfers between devices: none -> 5.63 us  [shards(): lax.all_to_all(jnp.stack(lax.axis_size('rows') * [m], 0), 'rows', split_a...]
    another operation x0 -> x1, local copies, waits for them, and re-layouts: none -> 2.49 us  [shards(): jnp.stack(lax.axis_size('rows') * [m], 0)]
  transfers between devices with their start and end apart: 2 -> 2, of which waited for: 2 -> 2; matrix products, arithmetic and copies ran while one was open for 3% -> 2% of each run, Pallas kernels for 0% -> 0%
where the time goes in v1:
time: 216 us
  waiting for transfers between devices  112 us (52%)
  blocking collectives  39.5 us (18%)
  matrix products  37 us (17%)
  starting transfers between devices  14.1 us (7%)
  local copies, waits for them, and re-layouts  11.2 us (5%)
    all_to_all x1, waiting for transfers between devices, shards(): lax.all_to_all(jnp.stack(lax.axis_size('rows') * [m], 0), 'rows', split_a...  85.3 us
    all_to_all x1, blocking collectives, shards(): lax.all_to_all(turned, 'rows', split_axis=1, concat_axis=1, tiled=True)  39.5 us
    all_to_all x1, waiting for transfers between devices, shards(): lax.all_to_all(jnp.stack([spectral_re, spectral_im]), 'rows', split_axis=...  26.3 us
    all_to_all x1, starting transfers between devices, shards(): lax.all_to_all(jnp.stack([spectral_re, spectral_im]), 'rows', split_axis=...  8.5 us
    dot_general x1, matrix products, shards(): jnp.einsum('ud,dkrc->ukrc', member, every, precision=lax.Precision.HIGHEST)  5.82 us
    all_to_all x1, starting transfers between devices, shards(): lax.all_to_all(jnp.stack(lax.axis_size('rows') * [m], 0), 'rows', split_a...  5.63 us
    dot_general x5, matrix products, exact_mix(): jnp.einsum(pattern, left_im, right_re, precision=highest)  5.04 us
    dot_general x5, matrix products, exact_mix(): jnp.einsum(pattern, left_im, right_im, precision=highest)  5.02 us
  transfers between devices with their start and end apart: 2, of which 2 were waited for; matrix products, arithmetic and copies ran while one was open for 2% of the time, Pallas kernels for 0%

profile of v1, /device:TPU:2, one launch (start us, length us, event | category | flops | bytes accessed | tf_op | source)
XLA Modules:
  0.0 215.8 jit_solution(11649410760760113087)
XLA Ops:
  2.1 1.0 multiply_add_fusion.2
  4.9 0.9 convolution_add_fusion.5
  6.0 1.0 add_bitcast_fusion
  7.8 39.5 %all_to_all.15 = f32[2,32,32,128]{3,2,0,1:T(8,128)S(1)} all-to-all(f32[2,32,32,128]{3,2,0,1:T(8,128)S(1)} %copy.93), channel_id=1, replica_groups=mesh['rows'=32,'rhs'=8] {'rows'}, dimensions={1} | all-to-all | bytes 2097152 | tf_op jit(solution)/shard_map/all_to_all | solution.py:90
  53.3 2.5 %stack.60 = f32[32,1,2,128,128]{4,3,2,1,0:T(8,128)} broadcast(f32[2,128,128]{2,1,0:T(8,128)S(1)} %copy.110), dimensions={2,3,4} | broadcast | bytes 4325376 | tf_op jit(solution)/shard_map/stack | solution.py:121
  55.8 5.6 %all-to-all-start.1 = ((f32[32,1,2,128,128]{4,3,2,1,0:T(8,128)}), f32[32,1,2,128,128]{4,3,2,1,0:T(8,128)}, u32[]{:S(2)}, u32[]{:S(2)}) async-start(f32[32,1,2,128,128]{4,3,2,1,0:T(8,128)} %stack.60), calls=%async_computation.1 | async-start | bytes 8388608 | tf_op jit(solution)/shard_map/all_to_all | solution.py:120
  61.7 1.4 copy-done.1
  63.1 0.9 convolution_bitcast_fusion.6
  64.0 0.9 convolution_bitcast_fusion.2
  65.6 1.2 convolution_subtract_fusion.6
  66.8 1.1 convolution_add_fusion.6
  67.9 85.3 %all-to-all-done.1 = f32[32,1,2,128,128]{4,3,2,1,0:T(8,128)} async-done(((f32[32,1,2,128,128]{4,3,2,1,0:T(8,128)}), f32[32,1,2,128,128]{4,3,2,1,0:T(8,128)}, u32[]{:S(2)}, u32[]{:S(2)}) %all-to-all-start.1) | async-done | bytes 4194336 | tf_op jit(solution)/shard_map/all_to_all | solution.py:120
  153.2 5.8 %fusion.6 = bf16[5,2,128,128]{3,0,2,1:T(8,128)(2,1)S(1)} fusion(f32[32,1,2,128,128]{4,3,2,1,0:T(8,128)} %all-to-all-done.1, f32[5]{0:T(128)S(1)} %copy-done.17, s32[5]{0:T(128)S(1)} %shift-right-arithmetic_xor_fusion), kind=kOutput, calls=%fused_computation.4 | convolution fusion | flops 63242560 | bytes 4522024 | tf_op jit(solution)/shard_map/ud,dkrc->ukrc/dot_general | solution.py:131
  163.6 1.0 fusion.12
  164.6 1.2 copy.124
  167.6 0.9 fusion.9
  168.6 1.6 copy.128
  170.2 8.5 %all-to-all-start.2 = ((f32[2,32,32,128]{3,2,0,1:T(8,128)}), f32[2,32,32,128]{3,2,0,1:T(8,128)S(1)}, u32[]{:S(2)}, u32[]{:S(2)}) async-start(f32[2,32,32,128]{3,2,0,1:T(8,128)} %copy.128), calls=%async_computation.2 | async-start | bytes 2097152 | tf_op jit(solution)/shard_map/all_to_all | solution.py:159
  178.9 26.3 %all-to-all-done.2 = f32[2,32,32,128]{3,2,0,1:T(8,128)S(1)} async-done(((f32[2,32,32,128]{3,2,0,1:T(8,128)}), f32[2,32,32,128]{3,2,0,1:T(8,128)S(1)}, u32[]{:S(2)}, u32[]{:S(2)}) %all-to-all-start.2) | async-done | bytes 1048608 | tf_op jit(solution)/shard_map/all_to_all | solution.py:159
  205.2 1.3 fusion.104
  206.5 1.3 fusion.103
  207.8 1.3 convolution_subtract_fusion.1
  209.1 1.4 multiply_subtract_fusion
  214.8 1.1 maximum_multiply_fusion.1
  (99 shorter events, 22.0 us)
Async XLA Ops:
  0.0 1.0 copy-start
  51.0 1.0 copy-start.3
  55.8 97.4 %all-to-all-start.1 = ((f32[32,1,2,128,128]{4,3,2,1,0:T(8,128)}), f32[32,1,2,128,128]{4,3,2,1,0:T(8,128)}, u32[]{:S(2)}, u32[]{:S(2)}) async-start(f32[32,1,2,128,128]{4,3,2,1,0:T(8,128)} %stack.60), calls=%async_computation.1 | async-start | bytes 8388608 | tf_op jit(solution)/shard_map/all_to_all | solution.py:120
  61.4 1.6 copy-start.1
  61.5 3.5 %copy-start.2 = (bf16[4,2,256,256]{3,2,1,0:T(8,128)(2,1)S(1)}, bf16[4,2,256,256]{3,2,1,0:T(8,128)(2,1)}, u32[]{:S(2)}) copy-start(bf16[4,2,256,256]{3,2,1,0:T(8,128)(2,1)} %param.7) | copy-start | bytes 3145732
  61.6 3.7 %copy-start.7 = (bf16[2,2,128,128]{2,3,1,0:T(8,128)(2,1)}, bf16[2,2,128,128]{2,3,1,0:T(8,128)(2,1)S(1)}, u32[]{:S(2)}) copy-start(bf16[2,2,128,128]{2,3,1,0:T(8,128)(2,1)S(1)} %multiply_convert_fusion) | copy-start | bytes 393220
  61.6 4.0 %copy-start.9 = (bf16[2,2,128,128]{2,3,1,0:T(8,128)(2,1)}, bf16[2,2,128,128]{2,3,1,0:T(8,128)(2,1)S(1)}, u32[]{:S(2)}) copy-start(bf16[2,2,128,128]{2,3,1,0:T(8,128)(2,1)S(1)} %multiply_convert_fusion.1) | copy-start | bytes 393220
  61.7 4.0 %copy-start.11 = (bf16[2,2,128,128]{2,3,1,0:T(8,128)(2,1)}, bf16[2,2,128,128]{2,3,1,0:T(8,128)(2,1)S(1)}, u32[]{:S(2)}) copy-start(bf16[2,2,128,128]{2,3,1,0:T(8,128)(2,1)S(1)} %broadcast_in_dim.5) | copy-start | bytes 393220
  64.0 2.8 %copy-start.13 = (bf16[2,2,128,128]{2,3,1,0:T(8,128)(2,1)}, bf16[2,2,128,128]{2,3,1,0:T(8,128)(2,1)S(1)}, u32[]{:S(2)}) copy-start(bf16[2,2,128,128]{2,3,1,0:T(8,128)(2,1)S(1)} %broadcast_in_dim.4) | copy-start | bytes 393220
  65.6 87.6 %copy-start.17 = (f32[5]{0:T(128)S(1)}, f32[5]{0:T(128)}, u32[]{:S(2)}) copy-start(f32[5]{0:T(128)} %constant.88.clone) | copy-start | bytes 64
  159.8 1.1 copy-start.10
  159.9 1.1 copy-start.14
  159.9 1.1 copy-start.16
  160.2 1.1 copy-start.4
  160.6 1.0 copy-start.8
  160.6 1.0 copy-start.12
  160.6 1.1 copy-start.15
  161.0 1.2 copy-start.6
  162.2 1.4 copy-start.5
  170.2 34.9 %all-to-all-start.2 = ((f32[2,32,32,128]{3,2,0,1:T(8,128)}), f32[2,32,32,128]{3,2,0,1:T(8,128)S(1)}, u32[]{:S(2)}, u32[]{:S(2)}) async-start(f32[2,32,32,128]{3,2,0,1:T(8,128)} %copy.128), calls=%async_computation.2 | async-start | bytes 2097152 | tf_op jit(solution)/shard_map/all_to_all | solution.py:159
